TPU v7x, 512 devices: a whole 4x4x16 slice. The times are simulated.
512 devices in a mesh: stream: 32 (over x, y, core), ctx: 16 (over z).
Axes of the slice: x: 4, y: 4, z: 16, core: 2. Of those that a mesh axis runs over, the one named last changes fastest.
Arguments:
- new_queries: bfloat16 [4096, 8192], P('stream', 'ctx'), may hold values from -8 to 8
- new_keys: bfloat16 [4096, 1024], P('stream'), may hold values from -8 to 8
- new_values: bfloat16 [4096, 1024], P('stream'), may hold values from -6 to 6
- cache_keys: bfloat16 [131072, 1024], P(('stream', 'ctx')), may hold values from -8 to 8
- cache_values: bfloat16 [131072, 1024], P(('stream', 'ctx')), may hold values from -6 to 6
- new_counts: int32 [32], replicated, may hold values from 16 to 128, as said below
- ctx_lengths: int32 [32], replicated, may hold values from 2 to 4096, as said below
- offloads: int32 [8, 4], replicated, may hold values from 0 to 31, as said below
Outputs:
- mixed_rows: bfloat16 [4096, 8192], P('stream', 'ctx')
- hosted: bfloat16 [2048, 8192], P('stream', 'ctx')
Inputs may be any that keep to these rules, and one draw needn't show every extreme that they name: `new_counts`: some stream has all 128 rows live; every source stream of offloads has all 128 rows live. `ctx_lengths`: some stream uses all 4096 cached positions. `offloads`: the 8 sources are distinct streams and so are the 8 destinations; no stream is both. A run's blocks are 1 to 2, some run has 2, and first + blocks <= 4.
All inputs are finite; a program needn't handle non-finite values.
Results may differ from a plain program's by a relative error of at most 0.0095.
Values may be sent and summed in bfloat16 or wider, within the bound.
A program may use at most 64 MiB of HBM per device.

v0:
```python
import math

import jax
import jax.numpy as jnp
from jax import lax
from jax.sharding import PartitionSpec as P

HEADS = 64
KV = 8
HD = 128
BLK = 32
NEW = 128
CAP = 64


NEG = -1e30


def partial_softmax(queries, key_rows, value_rows, visible):
    scale = 1.0 / math.sqrt(HD)
    scores = (
        jnp.einsum("rkge,pke->rkgp", queries, key_rows, preferred_element_type=jnp.float32) * scale
    )
    allowed = visible[:, None, None, :]
    scores = jnp.where(allowed, scores, NEG)
    maxima = jnp.max(scores, axis=-1)
    weights = jnp.where(allowed, jnp.exp(scores - maxima[..., None]), 0.0)
    totals = jnp.sum(weights, axis=-1)
    weighted = jnp.einsum(
        "rkgp,pke->rkge",
        weights.astype(jnp.bfloat16),
        value_rows,
        preferred_element_type=jnp.float32,
    )
    return (weighted / jnp.maximum(totals, 1.0)[..., None], maxima, totals)


def merge_blocks(received):
    partials, maxima, totals = received
    largest = jnp.max(maxima, axis=0)
    scaled = totals * jnp.exp(maxima - largest)
    summed = jnp.sum(scaled, axis=0)
    sources_count, row_count, columns = partials.shape
    head_count = maxima.shape[2]
    blocks = partials.reshape(sources_count, row_count, head_count, columns // head_count).astype(
        jnp.float32
    )
    combined = jnp.sum(scaled[..., None] * blocks, axis=0)
    cache_out = (combined / summed[..., None]).reshape(row_count, columns).astype(jnp.bfloat16)
    return (cache_out, largest, summed)


def finish(cache_out, largest, summed, own_out, own_max, own_total):
    highest = jnp.maximum(largest, own_max)
    first_weight = summed * jnp.exp(largest - highest)
    second_weight = own_total * jnp.exp(own_max - highest)
    row_count, head_count = largest.shape
    cached = cache_out.reshape(row_count, head_count, HD).astype(jnp.float32)
    mixed = first_weight[..., None] * cached + second_weight[..., None] * own_out
    mixed = mixed / (first_weight + second_weight)[..., None]
    return mixed.reshape(row_count, head_count * HD).astype(jnp.bfloat16)


def own_attention(queries, local_keys, local_values, first_row, kv_dev):
    row_count = queries.shape[0]
    head_count = queries.shape[1] // HD
    grouped = queries.reshape(row_count, kv_dev, head_count // kv_dev, HD)
    key_rows = local_keys.reshape(local_keys.shape[0], kv_dev, HD)
    value_rows = local_values.reshape(local_values.shape[0], kv_dev, HD)
    query_rows = first_row + jnp.arange(row_count)
    causal = jnp.arange(key_rows.shape[0])[None, :] <= query_rows[:, None]
    own_out, own_max, own_total = partial_softmax(grouped, key_rows, value_rows, causal)
    return (
        own_out.reshape(row_count, head_count, HD),
        own_max.reshape(row_count, head_count),
        own_total.reshape(row_count, head_count),
    )


def extend_rows(source_rows, start):
    padding = jnp.zeros((CAP,) + source_rows.shape[1:], source_rows.dtype)
    return lax.dynamic_slice_in_dim(jnp.concatenate([source_rows, padding], axis=0), start, CAP, 0)


def guest_finish(received, guest_start, kv_dev):
    guest_queries, guest_keys, guest_values, guest_cache, guest_largest, guest_summed = received
    guest_out, guest_max, guest_total = own_attention(
        guest_queries, guest_keys, guest_values, guest_start, kv_dev
    )
    return finish(guest_cache, guest_largest, guest_summed, guest_out, guest_max, guest_total)


def local(
    new_queries, new_keys, new_values, cache_keys, cache_values, new_counts, ctx_lengths, offloads
):
    group_count = lax.axis_size("stream")
    stream_index = lax.axis_index("stream")
    shard_index = lax.axis_index("ctx")
    ctx_dev = cache_keys.shape[0]
    heads_dev = new_queries.shape[1] // HD
    per_kv = HEADS // KV
    kv_dev = max(1, heads_dev // per_kv)
    length = ctx_lengths[stream_index]
    everything = lax.all_gather(new_queries, "ctx", axis=1, tiled=True).reshape(NEW, KV, per_kv, HD)
    cached_keys = cache_keys.reshape(ctx_dev, KV, HD)
    cached_values = cache_values.reshape(ctx_dev, KV, HD)
    positions = shard_index * ctx_dev + jnp.arange(ctx_dev)
    visible = jnp.broadcast_to((positions < length)[None, :], (NEW, ctx_dev))

    def one_head(head_index):
        queries = lax.dynamic_slice_in_dim(everything, head_index, 1, 1)
        key_rows = lax.dynamic_slice_in_dim(cached_keys, head_index, 1, 1)
        value_rows = lax.dynamic_slice_in_dim(cached_values, head_index, 1, 1)
        partial_value, maxima, totals = partial_softmax(queries, key_rows, value_rows, visible)
        return (partial_value[:, 0].astype(jnp.bfloat16), maxima[:, 0], totals[:, 0])

    partials, maxima, totals = lax.map(one_head, jnp.arange(KV))
    partials = jnp.transpose(partials, (1, 0, 2, 3)).reshape(1, NEW, HEADS * HD)
    maxima = jnp.transpose(maxima, (1, 0, 2)).reshape(1, NEW, HEADS)
    totals = jnp.transpose(totals, (1, 0, 2)).reshape(1, NEW, HEADS)
    cache_out, largest, summed = merge_blocks(
        (
            lax.all_to_all(
                partials.astype(jnp.float32), "ctx", split_axis=2, concat_axis=0, tiled=True
            ).astype(partials.dtype),
            lax.all_to_all(maxima, "ctx", split_axis=2, concat_axis=0, tiled=True),
            lax.all_to_all(totals, "ctx", split_axis=2, concat_axis=0, tiled=True),
        )
    )
    kv_first = shard_index * heads_dev // per_kv
    local_keys = lax.dynamic_slice_in_dim(new_keys, kv_first * HD, kv_dev * HD, 1)
    local_values = lax.dynamic_slice_in_dim(new_values, kv_first * HD, kv_dev * HD, 1)
    own_out, own_max, own_total = own_attention(new_queries, local_keys, local_values, 0, kv_dev)
    result = finish(cache_out, largest, summed, own_out, own_max, own_total)
    row_ids = jnp.arange(NEW)
    sources = offloads[:, 0]
    targets = offloads[:, 1]
    starts = offloads[:, 2] * BLK
    spans = offloads[:, 3] * BLK
    outgoing = sources == stream_index
    inside = (row_ids[None, :] >= starts[:, None]) & (row_ids[None, :] < (starts + spans)[:, None])
    handed = jnp.any(outgoing[:, None] & inside, axis=0)
    retained = (row_ids < new_counts[stream_index]) & jnp.logical_not(handed)
    mixed_rows = jnp.where(retained[:, None], result, 0.0)
    send_start = jnp.sum(jnp.where(outgoing, starts, 0))
    wanted = targets == stream_index
    has_guest = jnp.any(wanted)
    guest_source = jnp.sum(jnp.where(wanted, sources, 0))
    guest_start = jnp.sum(jnp.where(wanted, starts, 0))
    guest_span = jnp.sum(jnp.where(wanted, spans, 0))
    send_queries = extend_rows(new_queries, send_start)
    send_cache = extend_rows(cache_out, send_start)
    send_largest = extend_rows(largest, send_start)
    send_summed = extend_rows(summed, send_start)
    gathered = (
        lax.all_gather(send_queries.astype(jnp.float32), "stream", axis=0, tiled=True).astype(
            send_queries.dtype
        ),
        lax.all_gather(local_keys.astype(jnp.float32), "stream", axis=0, tiled=True).astype(
            local_keys.dtype
        ),
        lax.all_gather(local_values.astype(jnp.float32), "stream", axis=0, tiled=True).astype(
            local_values.dtype
        ),
        lax.all_gather(send_cache.astype(jnp.float32), "stream", axis=0, tiled=True).astype(
            send_cache.dtype
        ),
        lax.all_gather(send_largest, "stream", axis=0, tiled=True),
        lax.all_gather(send_summed, "stream", axis=0, tiled=True),
    )
    received = tuple(
        (
            lax.dynamic_slice_in_dim(
                member,
                guest_source * (member.shape[0] // group_count),
                member.shape[0] // group_count,
                0,
            )
            for member in gathered
        )
    )
    guest_result = guest_finish(received, guest_start, kv_dev)
    guest_keep = has_guest & (jnp.arange(CAP) < guest_span)
    hosted = jnp.where(guest_keep[:, None], guest_result, 0.0)
    return (mixed_rows, hosted)


def solution(mesh):
    placed = (
        P("stream", "ctx"),
        P("stream", None),
        P("stream", None),
        P(("stream", "ctx"), None),
        P(("stream", "ctx"), None),
        P(),
        P(),
        P(),
    )
    return jax.shard_map(
        local,
        mesh=mesh,
        in_specs=placed,
        out_specs=(P("stream", "ctx"), P("stream", "ctx")),
        check_vma=False,
    )
```

profile of v0, /device:TPU:1, one launch (start us, length us, event | category | flops | bytes accessed | tf_op | source)
XLA Modules:
  0.0 418.6 jit_solution(11617259261964962824)
XLA Ops:
  8.1 1.7 copy.117
  9.8 1.2 copy.115
  11.0 1.2 copy.116
  12.3 0.6 dynamic_slice.56
  12.9 0.6 add_compare_fusion
  13.5 67.4 %all-gather.8.cloned.1.call-done = bf16[128,8192]{0,1:T(8,128)(2,1)} async-done(((bf16[128,512]{0,1:T(8,128)(2,1)}), bf16[128,8192]{0,1:T(8,128)(2,1)}) %all-gather.8.cloned.1.call-update) | async-done | bytes 2097168 | tf_op jit(solution)/shard_map/all_gather | solution.py:104
  80.9 40.2 %while.15 = (s32[]{:T(128)}, bf16[8,128,8,128]{1,3,2,0:T(8,128)(2,1)S(1)}, f32[8,128,8]{1,2,0:T(8,128)}, f32[8,128,8]{1,2,0:T(8,128)}, s32[8]{0:T(128)S(1)}, /*i...) while((s32[]{:T(128)}, ...), condition=%wide.region_4.5_spmd.clone, body=%wide.region_1.4_spmd.clone.sunk | while | flops 136838144 | bytes 3849131 | solution.py:117
  83.4 1.3 fusion.109
  85.3 0.6 bitcast_dynamic-update-slice_fusion.3
  88.4 1.3 fusion.109
  90.3 0.6 bitcast_dynamic-update-slice_fusion.3
  93.5 1.3 fusion.109
  98.5 1.3 fusion.109
  100.4 0.6 bitcast_dynamic-update-slice_fusion.3
  103.5 1.3 fusion.109
  105.4 0.6 bitcast_dynamic-update-slice_fusion.3
  108.5 1.3 fusion.109
  110.4 0.6 bitcast_dynamic-update-slice_fusion.3
  113.5 1.3 fusion.109
  118.6 1.3 fusion.109
  121.1 6.5 %all-to-all-start.1 = ((f32[1,128,64]{1,0,2:T(1,128)}), f32[1,128,64]{1,0,2:T(1,128)S(1)}, u32[]{:S(2)}, u32[]{:S(2)}) async-start(f32[1,128,64]{1,0,2:T(1,128)} %bitcast.14), calls=%async_computation.1 | async-start | bytes 65536 | tf_op jit(solution)/shard_map/all_to_all | solution.py:126
  127.6 0.6 dynamic-slice_convert_fusion.4
  128.3 2.5 convert_element_type.130
  130.7 8.3 %all-to-all-done.1 = f32[1,128,64]{1,0,2:T(1,128)S(1)} async-done(((f32[1,128,64]{1,0,2:T(1,128)}), f32[1,128,64]{1,0,2:T(1,128)S(1)}, u32[]{:S(2)}, u32[]{:S(2)}) %all-to-all-start.1) | async-done | bytes 32800 | tf_op jit(solution)/shard_map/all_to_all | solution.py:126
  139.0 3.5 all-to-all-start
  142.5 7.7 %convert_bitcast_fusion = bf16[8192,1,128]{2,1,0:T(2,128)(2,1)} fusion(f32[1,128,8192]{1,0,2:T(1,128)} %bitcast.258), kind=kLoop, calls=%fused_computation.148 | loop fusion | flops 1048576 | bytes 6291456
  150.8 45.2 %reduce.9 = bf16[8192,128]{1,0:T(8,128)(2,1)S(1)} reduce(bf16[8192,1,128]{2,1,0:T(2,128)(2,1)} %convert_bitcast_fusion, bf16[]{:T(256)} %broadcast.156), dimensions={1}, to_apply=%convert_bitcast_fusion.reduce_sub_computation | reduce | bytes 4194306
  195.9 2.1 reshape.322
  198.0 11.5 %all-to-all-start.2 = ((bf16[16,2,32768]{2,1,0:T(2,128)(2,1)}), bf16[16,2,32768]{2,1,0:T(2,128)(2,1)S(1)}, u32[]{:S(2)}, u32[]{:S(2)}) async-start(bf16[16,2,32768]{2,1,0:T(2,128)(2,1)} %reshape.322), calls=%async_computation.2 | async-start | bytes 4194304 | tf_op jit(solution)/shard_map/all_to_all | solution.py:123
  209.6 0.7 fusion.84
  212.3 0.7 fusion.51
  213.1 0.8 constant_dynamic-slice_fusion.2
  213.8 0.7 copy.144
  215.3 0.7 not_and_fusion
  217.2 78.8 %all-to-all-done.2 = bf16[16,2,32768]{2,1,0:T(2,128)(2,1)S(1)} async-done(((bf16[16,2,32768]{2,1,0:T(2,128)(2,1)}), bf16[16,2,32768]{2,1,0:T(2,128)(2,1)S(1)}, u32[]{:S(2)}, u32[]{:S(2)}) %all-to-all-start.2) | async-done | bytes 2097184 | tf_op jit(solution)/shard_map/all_to_all | solution.py:123
  296.0 6.8 %reshape.323 = bf16[8192,1,128]{2,1,0:T(2,128)(2,1)} reshape(bf16[16,2,32768]{2,1,0:T(2,128)(2,1)S(1)} %all-to-all-done.2) | data formatting | bytes 4194304
  302.7 7.0 %bitcast_convert_fusion = f32[1,128,8192]{1,0,2:T(1,128)S(1)} fusion(bf16[8192,1,128]{2,1,0:T(2,128)(2,1)} %reshape.323), kind=kLoop, calls=%fused_computation.147 | loop fusion | flops 1048576 | bytes 6291456 | tf_op jit(solution)/shard_map/convert_element_type | solution.py:45
  311.0 0.8 broadcast_select_fusion
  311.8 0.7 fusion.52
  313.8 0.7 reduce_or.19
  314.6 0.6 iota_add_fusion
  315.2 1.3 compare_and_fusion
  316.7 32.1 %all-gather = f32[32,64,4]{1,2,0:T(4,128)S(1)} all-gather(f32[1,64,4]{1,2,0:T(4,128)S(1)} %fusion.79), channel_id=1, replica_groups=mesh['stream'=32,'ctx'=16] {'stream'}, dimensions={0}, use_global_device_ids=true | all-gather | bytes 33792 | tf_op jit(solution)/shard_map/all_gather | solution.py:169
  349.0 23.4 %all-gather.1 = f32[32,64,4]{1,2,0:T(4,128)S(1)} all-gather(f32[1,64,4]{1,2,0:T(4,128)S(1)} %fusion.80), channel_id=1, replica_groups=mesh['stream'=32,'ctx'=16] {'stream'}, dimensions={0}, use_global_device_ids=true | all-gather | bytes 33792 | tf_op jit(solution)/shard_map/all_gather | solution.py:168
  372.6 1.1 fusion.98
  374.0 1.0 fusion.30
  375.4 33.7 %all-gather.14.cloned.1.call-done = bf16[2048,512]{1,0:T(8,128)(2,1)} async-done(((bf16[64,512]{1,0:T(8,128)(2,1)}), bf16[2048,512]{1,0:T(8,128)(2,1)}) %all-gather.14.cloned.1.call-update) | async-done | bytes 2097168 | tf_op jit(solution)/shard_map/all_gather | solution.py:165
  409.5 1.6 broadcast_select_fusion.1
  (102 shorter events, 16.5 us)
Async XLA Ops:
  8.0 119.6 %copy-start = (bf16[128,1024]{1,0:T(8,128)(2,1)S(1)}, bf16[128,1024]{1,0:T(8,128)(2,1)}, u32[]{:S(2)}) copy-start(bf16[128,1024]{1,0:T(8,128)(2,1)} %param.11) | copy-start | bytes 786436
  8.0 4.3 %copy-start.3 = (s32[32]{0:T(128)S(1)}, s32[32]{0:T(128)}, u32[]{:S(2)}) copy-start(s32[32]{0:T(128)} %param.16) | copy-start | bytes 388
  8.0 72.9 %all-gather.8.cloned.1.call-start = ((), (), s32[]{:S(2)}) async-start(), calls=%async_computation.3 | async-start | bytes 2228224 | tf_op jit(solution)/shard_map/all_gather | solution.py:104
  121.1 18.0 %all-to-all-start.1 = ((f32[1,128,64]{1,0,2:T(1,128)}), f32[1,128,64]{1,0,2:T(1,128)S(1)}, u32[]{:S(2)}, u32[]{:S(2)}) async-start(f32[1,128,64]{1,0,2:T(1,128)} %bitcast.14), calls=%async_computation.1 | async-start | bytes 65536 | tf_op jit(solution)/shard_map/all_to_all | solution.py:126
  127.5 245.0 %all-gather.10.cloned.1.call-start = ((), (), s32[]{:S(2)}) async-start(), calls=%async_computation.4 | async-start | bytes 1081344 | tf_op jit(solution)/shard_map/all_gather | solution.py:159
  139.0 59.0 %all-to-all-start = ((f32[1,128,64]{1,0,2:T(1,128)}), f32[1,128,64]{1,0,2:T(1,128)S(1)}, u32[]{:S(2)}, u32[]{:S(2)}) async-start(f32[1,128,64]{1,0,2:T(1,128)} %bitcast.9), calls=%async_computation | async-start | bytes 65536 | tf_op jit(solution)/shard_map/all_to_all | solution.py:127
  198.0 11.6 %copy-start.2 = (s32[8,4]{0,1:T(4,128)S(1)}, s32[8,4]{0,1:T(4,128)}, u32[]{:S(2)}) copy-start(s32[8,4]{0,1:T(4,128)} %param.17) | copy-start | bytes 388
  198.0 14.3 %copy-start.1 = (bf16[128,512]{1,0:T(8,128)(2,1)S(1)}, bf16[128,512]{1,0:T(8,128)(2,1)}, u32[]{:S(2)}) copy-start(bf16[128,512]{1,0:T(8,128)(2,1)} %param.10) | copy-start | bytes 393220
  198.0 16.6 %copy-start.4 = (s32[32]{0:T(128)S(1)}, s32[32]{0:T(128)}, u32[]{:S(2)}) copy-start(s32[32]{0:T(128)} %param.15) | copy-start | bytes 388
  198.0 97.9 %all-to-all-start.2 = ((bf16[16,2,32768]{2,1,0:T(2,128)(2,1)}), bf16[16,2,32768]{2,1,0:T(2,128)(2,1)S(1)}, u32[]{:S(2)}, u32[]{:S(2)}) async-start(bf16[16,2,32768]{2,1,0:T(2,128)(2,1)} %reshape.322), calls=%async_computation.2 | async-start | bytes 4194304 | tf_op jit(solution)/shard_map/all_to_all | solution.py:123
  209.6 163.0 %all-gather.12.cloned.1.call-start = ((), (), s32[]{:S(2)}) async-start(), calls=%async_computation.5 | async-start | bytes 2162688 | tf_op jit(solution)/shard_map/all_gather | solution.py:156
  213.0 161.0 %all-gather.16.cloned.1.call-start = ((), (), s32[]{:S(2)}) async-start(), calls=%async_computation.7 | async-start | bytes 1081344 | tf_op jit(solution)/shard_map/all_gather | solution.py:162
  214.6 194.5 %all-gather.14.cloned.1.call-start = ((), (), s32[]{:S(2)}) async-start(), calls=%async_computation.6 | async-start | bytes 2162688 | tf_op jit(solution)/shard_map/all_gather | solution.py:165
Sparse Core Ops, SparseCore 0:
  11.5 69.3 all-gather.7
Sparse Core Ops, SparseCore 1:
  131.2 70.1 all-gather.9
  213.8 72.8 all-gather.11
  289.5 57.7 all-gather.15
  350.4 58.6 all-gather.13
where the time goes:
time: 420 us; the launch traced here: 419 us
  waiting for transfers between devices  188 us (45%)
  other arithmetic  72 us (17%)
  blocking collectives  55.6 us (13%)
  local copies, waits for them, and re-layouts  30.3 us (7%)
  starting transfers between devices  21.7 us (5%)
  between operations  19.3 us (5%)
  loops' own time  15.8 us (4%)
  matrix products  15.6 us (4%)
    all_to_all x1, waiting for transfers between devices, local(): lax.all_to_all(partials.astype(jnp.float32), 'ctx', split_axis=2, concat_...  78.8 us
    all_gather x1, waiting for transfers between devices, local(): lax.all_gather(new_queries, 'ctx', axis=1, tiled=True)  67.4 us
    unnamed x2, other arithmetic  52.9 us
    all_gather x1, waiting for transfers between devices, local(): lax.all_gather(send_cache.astype(jnp.float32), 'stream', axis=0, tiled=True)  33.7 us
    all_gather x1, blocking collectives, local(): lax.all_gather(send_summed, 'stream', axis=0, tiled=True)  32.1 us
    all_gather x1, blocking collectives, local(): lax.all_gather(send_largest, 'stream', axis=0, tiled=True)  23.4 us
    another operation x1, loops' own time, local(): partials, maxima, totals = lax.map(one_head, jnp.arange(KV))  15.8 us
    unnamed x21, local copies, waits for them, and re-layouts  14.6 us
  transfers between devices with their start and end apart: 8, of which 4 were waited for; matrix products, arithmetic and copies ran while one was open for 21% of the time, Pallas kernels for 0%

commit v1 on v0

v1 whole, which is shorter than its diff:
```python
import functools
import math

import jax
import jax.numpy as jnp
from jax import lax
from jax.experimental import pallas as pl
from jax.experimental.pallas import tpu as pltpu
from jax.sharding import PartitionSpec as P

HEADS = 64
KV = 8
HD = 128
BLK = 32
NEW = 128
CAP = 64
RUNS = 8
N_CTX = 16
N_STREAM = 32
CHIPS = N_STREAM // 2
SIDE = N_CTX // 2
REACH = 3
FAR = SIDE - 1 - REACH
HALF = NEW // 2
QROWS = 4 * HALF
PACK = HD + 16

NEG = -(2.0**100)
LOG2_SCALE = math.log2(math.e) / math.sqrt(HD)
MESH = pl.DeviceIdType.MESH


def merge(first, second):
    acc_a, max_a, tot_a = first
    acc_b, max_b, tot_b = second
    top = jnp.maximum(max_a, max_b)
    scale_a = jnp.exp2(max_a - top)
    scale_b = jnp.exp2(max_b - top)
    return (acc_a * scale_a + acc_b * scale_b, top, tot_a * scale_a + tot_b * scale_b)


def attend(keys, values_t, queries, allowed):
    scores = lax.dot_general(
        keys, queries, (((1,), (1,)), ((), ())), preferred_element_type=jnp.float32
    )
    scores = jnp.where(allowed, scores * LOG2_SCALE, NEG)
    top = jnp.max(scores, axis=0, keepdims=True).astype(jnp.bfloat16).astype(jnp.float32)
    weights = jnp.exp2(scores - top)
    total = jnp.sum(weights, axis=0, keepdims=True)
    acc = jnp.dot(values_t, weights.astype(jnp.bfloat16), preferred_element_type=jnp.float32)
    return acc, top, total


def pack_rows(top, total):
    high = total.astype(jnp.bfloat16).astype(jnp.float32)
    low = total - high
    width = top.shape[1]
    row = lax.broadcasted_iota(jnp.int32, (16, width), 0)
    rows = jnp.where(row == 0, top, jnp.where(row == 1, high, jnp.where(row == 2, low, 0.0)))
    return rows.astype(jnp.bfloat16)


def unpack(packed):
    stats = packed[HD:PACK, :].astype(jnp.float32)
    return packed[:HD, :].astype(jnp.float32), stats[0:1], stats[1:2] + stats[2:3]


def kernel(
    counts_ref, lengths_ref, offloads_ref,
    q_hbm, nk_hbm, nv_hbm, ck_hbm, cv_hbm,
    mixed_ref, hosted_ref,
    q_in, nk, nv, ck, cv, vt, qbuf, kbuf, vbuf, acc_ref, stat_ref, osend, orecv, psend, precv,
    fin_f, run, p1, p3, host,
    in_sem, kv_s, kv_r, q_s, q_r, o_s, o_r, p_s, p_r, p1_s, p1_r, p2_s, p2_r, p3_s, p3_r,
):
    s = lax.axis_index("stream")
    t = lax.axis_index("ctx")
    core = lax.rem(s, 2)
    chip = s // 2
    side = 1 - 2 * lax.rem(t, 2)

    def ring(v):
        return lax.rem(v + 2 * N_CTX, N_CTX)

    def inward(i):
        return side if i % 2 == 0 else -side

    def near(i):
        return ring(t + inward(i) * i)

    def head(i):
        return near(i) // 2

    def columns(i):
        return pl.ds(pl.multiple_of(head(i) * HD, HD), HD)

    own_kv = pl.ds(pl.multiple_of((t // 2) * HD, HD), HD)
    loads = [
        pltpu.make_async_copy(q_hbm, q_in, in_sem.at[0]),
        pltpu.make_async_copy(ck_hbm, ck, in_sem.at[1]),
        pltpu.make_async_copy(cv_hbm, cv, in_sem.at[2]),
        pltpu.make_async_copy(nk_hbm.at[:, own_kv], nk, in_sem.at[3]),
        pltpu.make_async_copy(nv_hbm.at[:, own_kv], nv, in_sem.at[4]),
    ]
    barrier = pltpu.get_barrier_semaphore()
    reach = max(FAR, 1)
    greeted = 0
    for k in range(1, reach + 1):
        for sign in (1, -1):
            pl.semaphore_signal(barrier, inc=1, device_id=(s, ring(t + sign * k)), device_id_type=MESH)
            greeted += 1
    for k in range(1, CHIPS):
        peer = 2 * lax.rem(chip + k, CHIPS) + core
        pl.semaphore_signal(barrier, inc=1, device_id=(peer, t), device_id_type=MESH)
        greeted += 1
    sibling = s + 1 - 2 * core
    pl.semaphore_signal(barrier, inc=1, device_id=(sibling, t), device_id_type=MESH)
    greeted += 1
    for copy in loads:
        copy.start()

    out_first = jnp.int32(0)
    out_span = jnp.int32(0)
    in_span = jnp.int32(0)
    for i in range(RUNS):
        mine = offloads_ref[i, 0] == s
        out_first += jnp.where(mine, offloads_ref[i, 2], 0)
        out_span += jnp.where(mine, offloads_ref[i, 3] * BLK, 0)
        in_span += jnp.where(offloads_ref[i, 1] == s, offloads_ref[i, 3] * BLK, 0)
    count = counts_ref[s]
    length = lengths_ref[s]
    first = jnp.minimum(out_first, 2)
    rest_a = jnp.where(first == 0, 2, 0)
    rest_b = jnp.where(first == 2, 1, 3)
    order = ((first, first + 1), (rest_a, rest_b))
    out_start = out_first * BLK

    loads[0].wait()
    for h in range(2):
        for part in range(2):
            rows = q_in[order[h][part]]
            for n in range(4):
                lo = n * HALF + part * BLK
                qbuf[0, 0, h, lo : lo + BLK, :] = rows[:, n * HD : (n + 1) * HD]
    loads[1].wait()
    loads[2].wait()
    pl.semaphore_wait(barrier, greeted)

    def remote(src, dst, send, recv, device):
        return pltpu.make_async_remote_copy(
            src_ref=src, dst_ref=dst, send_sem=send, recv_sem=recv, device_id=device, device_id_type=MESH
        )

    def kv_copies(i):
        target = (s, ring(t + inward(i) * (i - REACH)))
        slot = i - REACH - 1
        return (
            remote(ck.at[:, columns(i)], kbuf.at[slot], kv_s.at[0, slot], kv_r.at[0, slot], target),
            remote(cv.at[:, columns(i)], vbuf.at[slot], kv_s.at[1, slot], kv_r.at[1, slot], target),
        )

    def q_partner(h):
        return remote(
            qbuf.at[0, 0, h], qbuf.at[0, 1, h], q_s.at[0, 2, h], q_r.at[0, 1, h], (s, ring(t + inward(0)))
        )

    def q_outward(i, o, h):
        return remote(
            qbuf.at[i, o, h], qbuf.at[i + 1, o, h], q_s.at[i, o, h], q_r.at[i + 1, o, h],
            (s, ring(t - inward(i))),
        )

    def q_arrival(i, o, h):
        return q_partner(h) if i == 0 else q_outward(i - 1, o, h)

    def out_inward(i, h):
        return remote(
            osend.at[i - 1, h], orecv.at[i - 1, h], o_s.at[i - 1, h], o_r.at[i - 1, h],
            (s, ring(t + inward(i))),
        )

    def out_partner(h):
        return remote(psend.at[h], precv.at[h], p_s.at[h], p_r.at[h], (s, ring(t + inward(0))))

    def wait_arrival(i, o, h):
        q_arrival(i, o, h).wait_recv()

    started = []

    def go(copy):
        copy.start()
        started.append(copy)

    for h in range(1):
        go(q_partner(h))
        go(q_outward(0, 0, h))
    for i in range(REACH + 1, SIDE):
        for copy in kv_copies(i):
            go(copy)
    for h in range(1, 2):
        go(q_partner(h))
        go(q_outward(0, 0, h))

    loads[3].wait()
    loads[4].wait()
    nvt = nv[...].T
    lane = lax.broadcasted_iota(jnp.int32, (NEW, QROWS), 1)
    key_row = lax.broadcasted_iota(jnp.int32, (NEW, QROWS), 0)
    in_half = lax.rem(lane, HALF)
    own = []
    for h in range(2):
        row_id = jnp.where(
            in_half < BLK, order[h][0] * BLK + in_half, order[h][1] * BLK + in_half - BLK
        )
        own.append(attend(nk[...], nvt, qbuf[0, 0, h], key_row <= row_id))
    for i in range(REACH + 1):
        vt[i] = cv[:, columns(i)].T

    position = lax.broadcasted_iota(jnp.int32, (2 * N_CTX * 8, 2 * QROWS), 0)

    def keep(i, h, state):
        acc_ref[i, h] = state[0]
        stat_ref[i, h, 0:1, :] = state[1]
        stat_ref[i, h, 1:2, :] = state[2]

    def held(i, h):
        return acc_ref[i, h], stat_ref[i, h, 0:1, :], stat_ref[i, h, 1:2, :]

    def queries(i, h):
        return jnp.concatenate([qbuf[i, 0, h], qbuf[i, 1, h]], axis=0)

    def own_block(i, h):
        allowed = position < length - t * 256
        keep(i, h, attend(ck[:, columns(i)], vt[i], queries(i, h), allowed))

    def arrive(step, h):
        for i in range(REACH + 1):
            o = step - i
            if o in (0, 1) and (i, o) != (0, 0):
                wait_arrival(i, o, h)
                if i < REACH:
                    go(q_outward(i, o, h))

    for step in range(1, REACH + 2):
        for h in range(2):
            arrive(step, h)
            own_block(step - 1, h)

    for i in range(REACH + 1, SIDE):
        slot = i - REACH - 1
        for copy in kv_copies(i):
            copy.wait_recv()
        source = ring(t - inward(REACH) * (slot + 1))
        far_vt = vbuf[slot].T
        for h in range(2):
            allowed = position < length - source * 256
            part = attend(kbuf[slot], far_vt, queries(REACH, h), allowed)
            keep(REACH, h, merge(held(REACH, h), part))

    for i in range(REACH, 0, -1):
        for h in range(2):
            state = held(i, h)
            if i < REACH:
                out_inward(i + 1, h).wait_recv()
                state = merge(state, unpack(orecv[i, h]))
            osend[i - 1, h, :HD, :] = state[0].astype(jnp.bfloat16)
            osend[i - 1, h, HD:PACK, :] = pack_rows(state[1], state[2])
            go(out_inward(i, h))
    mine = []
    for h in range(2):
        out_inward(1, h).wait_recv()
        acc, top, total = merge(held(0, h), unpack(orecv[0, h]))
        psend[h, :HD, :] = acc[:, QROWS:].astype(jnp.bfloat16)
        psend[h, HD:PACK, :] = pack_rows(top[:, QROWS:], total[:, QROWS:])
        go(out_partner(h))
        keep(0, h, (acc, top, total))

    def finish(h):
        out_partner(h).wait_recv()
        acc, top, total = held(0, h)
        state = merge((acc[:, :QROWS], top[:, :QROWS], total[:, :QROWS]), own[h])
        acc, top, total = merge(state, unpack(precv[h]))
        rows = (acc / total).T
        for n in range(4):
            for part in range(2):
                lo = n * HALF + part * BLK
                fin_f[2 * h + part, :, n * HD : (n + 1) * HD] = rows[lo : lo + BLK]

    finish(0)
    shifted = out_first > first
    run[:BLK, :] = jnp.where(shifted, fin_f[1], fin_f[0]).astype(jnp.bfloat16)
    run[BLK:, :] = fin_f[1].astype(jnp.bfloat16)

    def p1_copy(k):
        there = lax.rem(chip + k, CHIPS)
        piece = run.at[
            pl.ds(pl.multiple_of((there // 4) * 16, 16), 16), pl.ds(pl.multiple_of(lax.rem(there, 4) * HD, HD), HD)
        ]
        return remote(piece, p1.at[core * CHIPS + chip], p1_s.at[k], p1_r.at[k], (2 * there + core, t))

    def p1_arrival(k):
        here = lax.rem(chip + CHIPS - k, CHIPS)
        return remote(p1.at[core * CHIPS + here], p1.at[core * CHIPS + here], p1_s.at[k], p1_r.at[k], (2 * here + core, t))

    my_rows = pl.ds(pl.multiple_of((chip // 4) * 16, 16), 16)
    my_cols = pl.ds(pl.multiple_of(lax.rem(chip, 4) * HD, HD), HD)
    for k in range(1, CHIPS):
        go(p1_copy(k))
    p1[core * CHIPS + chip] = run[my_rows, my_cols]

    finish(1)
    row32 = lax.broadcasted_iota(jnp.int32, (BLK, 4 * HD), 0)
    for b in range(4):
        place = jnp.where(
            first == b, 0, jnp.where(first + 1 == b, 1, jnp.where(rest_a == b, 2, 3))
        )
        rows = fin_f[place]
        row = row32 + b * BLK
        retained = (row < count) & ((row < out_start) | (row >= out_start + out_span))
        mixed_ref[b * BLK : (b + 1) * BLK, :] = jnp.where(retained, rows, 0.0).astype(jnp.bfloat16)

    for k in range(1, CHIPS):
        p1_arrival(k).wait_recv()
    mine16 = p1.at[pl.ds(core * CHIPS, CHIPS)]
    other16 = p1.at[pl.ds((1 - core) * CHIPS, CHIPS)]
    go(remote(mine16, mine16, p2_s.at[0], p2_r.at[0], (sibling, t)))
    other = remote(other16, other16, p2_s.at[0], p2_r.at[0], (sibling, t))
    other.wait_recv()

    def p3_copy(k):
        there = lax.rem(chip + k, CHIPS)
        return remote(p3.at[k], host.at[my_rows, my_cols], p3_s.at[k], p3_r.at[k], (2 * there + core, t))

    def p3_arrival(k):
        here = lax.rem(chip + CHIPS - k, CHIPS)
        place = host.at[
            pl.ds(pl.multiple_of((here // 4) * 16, 16), 16), pl.ds(pl.multiple_of(lax.rem(here, 4) * HD, HD), HD)
        ]
        return remote(place, place, p3_s.at[k], p3_r.at[k], (2 * here + core, t))

    slots = [lax.rem(offloads_ref[i, 0], 2) * CHIPS + lax.div(offloads_ref[i, 0], 2) for i in range(RUNS)]
    for k in range(CHIPS):
        target = 2 * lax.rem(chip + k, CHIPS) + core
        source = jnp.int32(0)
        for i in range(RUNS):
            source += jnp.where(offloads_ref[i, 1] == target, slots[i], 0)
        piece = p1[source]
        if k == 0:
            host[my_rows, my_cols] = piece
        else:
            p3[k] = piece
            go(p3_copy(k))
    for k in range(1, CHIPS):
        p3_arrival(k).wait_recv()
    row64 = lax.broadcasted_iota(jnp.int32, (CAP, 4 * HD), 0)
    hosted_ref[...] = jnp.where(row64 < in_span, host[...].astype(jnp.float32), 0.0).astype(jnp.bfloat16)

    for copy in started:
        copy.wait_send()


def local(
    new_queries, new_keys, new_values, cache_keys, cache_values, new_counts, ctx_lengths, offloads
):
    bf16, f32 = jnp.bfloat16, jnp.float32
    dma = pltpu.SemaphoreType.DMA
    smem = pl.BlockSpec(memory_space=pltpu.SMEM)
    anywhere = pl.BlockSpec(memory_space=pl.ANY)
    vmem = pl.BlockSpec(memory_space=pltpu.VMEM)
    far = max(FAR, 1)
    return pl.pallas_call(
        kernel,
        name="attend_and_relocate",
        out_shape=(
            jax.ShapeDtypeStruct((NEW, 4 * HD), bf16),
            jax.ShapeDtypeStruct((CAP, 4 * HD), bf16),
        ),
        in_specs=[smem] * 3 + [anywhere] * 5,
        out_specs=(vmem, vmem),
        scratch_shapes=[
            pltpu.VMEM((4, BLK, 4 * HD), bf16),
            pltpu.VMEM((NEW, HD), bf16),
            pltpu.VMEM((NEW, HD), bf16),
            pltpu.VMEM((256, KV * HD), bf16),
            pltpu.VMEM((256, KV * HD), bf16),
            pltpu.VMEM((REACH + 1, HD, 256), bf16),
            pltpu.VMEM((REACH + 1, 2, 2, QROWS, HD), bf16),
            pltpu.VMEM((far, 256, HD), bf16),
            pltpu.VMEM((far, 256, HD), bf16),
            pltpu.VMEM((REACH + 1, 2, HD, 2 * QROWS), f32),
            pltpu.VMEM((REACH + 1, 2, 8, 2 * QROWS), f32),
            pltpu.VMEM((REACH, 2, PACK, 2 * QROWS), bf16),
            pltpu.VMEM((REACH, 2, PACK, 2 * QROWS), bf16),
            pltpu.VMEM((2, PACK, QROWS), bf16),
            pltpu.VMEM((2, PACK, QROWS), bf16),
            pltpu.VMEM((4, BLK, 4 * HD), f32),
            pltpu.VMEM((CAP, 4 * HD), bf16),
            pltpu.VMEM((2 * CHIPS, 16, HD), bf16),
            pltpu.VMEM((CHIPS, 16, HD), bf16),
            pltpu.VMEM((CAP, 4 * HD), bf16),
            dma((5,)),
            dma((2, far)),
            dma((2, far)),
            dma((REACH + 1, 3, 2)),
            dma((REACH + 1, 2, 2)),
            dma((REACH, 2)),
            dma((REACH, 2)),
            dma((2,)),
            dma((2,)),
            dma((CHIPS,)),
            dma((CHIPS,)),
            dma((1,)),
            dma((1,)),
            dma((CHIPS,)),
            dma((CHIPS,)),
        ],
        compiler_params=pltpu.CompilerParams(
            collective_id=0, has_side_effects=True, vmem_limit_bytes=48 * 1024 * 1024
        ),
    )(new_counts, ctx_lengths, offloads, new_queries.reshape(4, BLK, 4 * HD), new_keys, new_values, cache_keys, cache_values)


def solution(mesh):
    placed = (
        P("stream", "ctx"),
        P("stream", None),
        P("stream", None),
        P(("stream", "ctx"), None),
        P(("stream", "ctx"), None),
        P(),
        P(),
        P(),
    )
    return jax.shard_map(
        local,
        mesh=mesh,
        in_specs=placed,
        out_specs=(P("stream", "ctx"), P("stream", "ctx")),
        check_vma=False,
    )
```

time: 420 us -> 87.9 us (0.21)
  waiting for transfers between devices: 188 us -> 0 us
  Pallas kernels: 0 us -> 80 us
  other arithmetic: 72 us -> 0 us
  blocking collectives: 55.6 us -> 0 us
  local copies, waits for them, and re-layouts: 30.3 us -> 6.95 us
  starting transfers between devices: 21.7 us -> 0 us
  between operations: 19.3 us -> 0.66 us
  loops' own time: 15.8 us -> 0 us
  matrix products: 15.6 us -> 0 us
    all_gather x5 -> x0, waiting for transfers between devices: 101 us -> none  [the longest x1 67.4 us: local(): lax.all_gather(new_queries, 'ctx', axis=1, tiled=True)]
    all_to_all x3 -> x0, waiting for transfers between devices: 87.1 us -> none  [the longest x1 78.8 us: local(): lax.all_to_all(partials.astype(jnp.float32), 'ctx', split_axis=2, concat_...]
    pallas_call x0 -> x1, Pallas kernels: none -> 80 us  [local(): pl.pallas_call(kernel, name='attend_and_relocate', out_shape=(jax.ShapeDt...]
    all_gather x2 -> x0, blocking collectives: 55.6 us -> none  [the longest x1 32.1 us: local(): lax.all_gather(send_summed, 'stream', axis=0, tiled=True)]
    unnamed x2 -> x0, other arithmetic: 52.9 us -> none
    all_to_all x3 -> x0, starting transfers between devices: 21.5 us -> none  [the longest x1 11.5 us: local(): lax.all_to_all(partials.astype(jnp.float32), 'ctx', split_axis=2, concat_...]
    another operation x1 -> x0, loops' own time: 15.8 us -> none  [local(): partials, maxima, totals = lax.map(one_head, jnp.arange(KV))]
    dot_general x20 -> x0, matrix products: 15.6 us -> none  [the longest x10 11.6 us: partial_softmax(): jnp.einsum('rkge,pke->rkgp', queries, key_rows, preferred_element_type=jn...]
  transfers between devices with their start and end apart: 8 -> 0, of which waited for: 4 -> 0; matrix products, arithmetic and copies ran while one was open for 21% -> 0% of each run, Pallas kernels for 0% -> 0%
where the time goes in v1:
time: 87.9 us; the launch traced here: 87.6 us
  Pallas kernels  80 us (91%)
  local copies, waits for them, and re-layouts  6.95 us (8%)
    pallas_call x1, Pallas kernels, local(): pl.pallas_call(kernel, name='attend_and_relocate', out_shape=(jax.ShapeDt...  80 us
    unnamed x17, local copies, waits for them, and re-layouts  6.95 us

profile of v1, /device:TPU:1, one launch (start us, length us, event | category | flops | bytes accessed | tf_op | source)
XLA Modules:
  0.0 87.6 jit_solution(4793983786669095226)
XLA Ops:
  0.6 0.0 copy-start.5
  0.6 0.0 copy-start.6
  0.7 0.8 copy.10.offloads_ref
  1.4 0.0 copy-done.5
  1.4 0.0 copy-done.6
  1.4 0.0 copy-start
  1.4 1.0 %copy-done = bf16[256,1024]{1,0:T(8,128)(2,1)S(1)} copy-done((bf16[256,1024]{1,0:T(8,128)(2,1)S(1)}, bf16[256,1024]{1,0:T(8,128)(2,1)}, u32[]{:S(2)}) %copy-start) | copy-done | bytes 524312
  2.5 0.0 copy-start.1
  2.5 1.0 %copy-done.1 = bf16[256,1024]{1,0:T(8,128)(2,1)S(1)} copy-done((bf16[256,1024]{1,0:T(8,128)(2,1)S(1)}, bf16[256,1024]{1,0:T(8,128)(2,1)}, u32[]{:S(2)}) %copy-start.1) | copy-done | bytes 524312
  3.5 0.0 copy-start.2
  3.5 0.9 %copy-done.2 = bf16[128,1024]{1,0:T(8,128)(2,1)S(1)} copy-done((bf16[128,1024]{1,0:T(8,128)(2,1)S(1)}, bf16[128,1024]{1,0:T(8,128)(2,1)}, u32[]{:S(2)}) %copy-start.2) | copy-done | bytes 262168
  4.5 0.0 copy-start.3
  4.5 0.9 %copy-done.3 = bf16[128,1024]{1,0:T(8,128)(2,1)S(1)} copy-done((bf16[128,1024]{1,0:T(8,128)(2,1)S(1)}, bf16[128,1024]{1,0:T(8,128)(2,1)}, u32[]{:S(2)}) %copy-start.3) | copy-done | bytes 262168
  5.4 0.0 copy-start.4
  5.4 0.9 %copy-done.4 = bf16[128,512]{1,0:T(8,128)(2,1)S(1)} copy-done((bf16[128,512]{1,0:T(8,128)(2,1)S(1)}, bf16[128,512]{1,0:T(8,128)(2,1)}, u32[]{:S(2)}) %copy-start.4) | copy-done | bytes 131096
  6.3 80.0 %attend_and_relocate.1 = (bf16[128,512]{1,0:T(8,128)(2,1)S(1)}, bf16[64,512]{1,0:T(8,128)(2,1)S(1)}) custom-call(s32[32]{0:T(128)S(1)} %copy-done.5, s32[32]{0:T(128)S(1)} %copy-done.6, s32[8,4]{1,0:T(8,128)S(1)} %copy.10.offloads_ref, bf16[4,32,512]{2,1,0:T(8,128)(2,1)S(1)} %bitcast.1, bf16[128,1024]{1,0:T(8,128)(2,1)S(1)} %copy-done.2, ...), custom_call_target="tpu_custom_call" | custom-call | tf_op jit(solution)/shard_map/attend_and_relocate/pallas_call | solution.py:371
  86.3 0.7 copy.13
  87.0 0.6 copy.14
Async XLA Ops:
  0.6 0.8 copy-start.5
  0.6 0.8 copy-start.6
  1.4 1.0 %copy-start = (bf16[256,1024]{1,0:T(8,128)(2,1)S(1)}, bf16[256,1024]{1,0:T(8,128)(2,1)}, u32[]{:S(2)}) copy-start(bf16[256,1024]{1,0:T(8,128)(2,1)} %ck_hbm.1) | copy-start | bytes 1572868
  2.5 1.0 %copy-start.1 = (bf16[256,1024]{1,0:T(8,128)(2,1)S(1)}, bf16[256,1024]{1,0:T(8,128)(2,1)}, u32[]{:S(2)}) copy-start(bf16[256,1024]{1,0:T(8,128)(2,1)} %cv_hbm.1) | copy-start | bytes 1572868
  3.5 0.9 %copy-start.2 = (bf16[128,1024]{1,0:T(8,128)(2,1)S(1)}, bf16[128,1024]{1,0:T(8,128)(2,1)}, u32[]{:S(2)}) copy-start(bf16[128,1024]{1,0:T(8,128)(2,1)} %nk_hbm.1) | copy-start | bytes 786436
  4.5 0.9 %copy-start.3 = (bf16[128,1024]{1,0:T(8,128)(2,1)S(1)}, bf16[128,1024]{1,0:T(8,128)(2,1)}, u32[]{:S(2)}) copy-start(bf16[128,1024]{1,0:T(8,128)(2,1)} %nv_hbm.1) | copy-start | bytes 786436
  5.4 0.9 %copy-start.4 = (bf16[128,512]{1,0:T(8,128)(2,1)S(1)}, bf16[128,512]{1,0:T(8,128)(2,1)}, u32[]{:S(2)}) copy-start(bf16[128,512]{1,0:T(8,128)(2,1)} %param.8) | copy-start | bytes 393220

commit v2 on v1

--- a/solution.py
+++ b/solution.py
@@ -19,8 +19,14 @@
 N_STREAM = 32
 CHIPS = N_STREAM // 2
 SIDE = N_CTX // 2
-REACH = 3
+REACH = 1
 FAR = SIDE - 1 - REACH
+KV_TURN = (0, 1, 2, 3, 4, 5, 6, 7)
+OFFSETS = sorted(
+    ((dx, dy) for dx in range(4) for dy in range(4)),
+    key=lambda d: -(min(d[0], 4 - d[0]) + min(d[1], 4 - d[1])),
+)
+OFFSETS = OFFSETS[-1:] + OFFSETS[:-1]
 HALF = NEW // 2
 QROWS = 4 * HALF
 PACK = HD + 16
@@ -28,6 +34,9 @@
 NEG = -(2.0**100)
 LOG2_SCALE = math.log2(math.e) / math.sqrt(HD)
 MESH = pl.DeviceIdType.MESH
+FIRST_QUERIES = (0, 1)
+SCHEDULE = (('arrive', 1, 0), ('arrive', 1, 1), ('own', 0, 0), ('own', 0, 1), ('arrive', 2, 0), ('arrive', 2, 1), ('own', 1, 0), ('own', 1, 1), ('far', 2, 0), ('far', 2, 1), ('far', 3, 0), ('far', 3, 1), ('far', 4, 0), ('far', 4, 1), ('far', 5, 0), ('far', 5, 1), ('far', 6, 0), ('far', 6, 1), ('far', 7, 0), ('out', 1, 0), ('far', 7, 1), ('out', 1, 1), ('pair', 0))
+LATE = (('pair', 1),)
 
 
 def merge(first, second):
@@ -69,7 +78,7 @@
     counts_ref, lengths_ref, offloads_ref,
     q_hbm, nk_hbm, nv_hbm, ck_hbm, cv_hbm,
     mixed_ref, hosted_ref,
-    q_in, nk, nv, ck, cv, vt, qbuf, kbuf, vbuf, acc_ref, stat_ref, osend, orecv, psend, precv,
+    q_in, nk, nv, ck, cv, vt, qbuf, kbuf, vbuf, far_vt, acc_ref, stat_ref, osend, orecv, psend, precv,
     fin_f, run, p1, p3, host,
     in_sem, kv_s, kv_r, q_s, q_r, o_s, o_r, p_s, p_r, p1_s, p1_r, p2_s, p2_r, p3_s, p3_r,
 ):
@@ -83,13 +92,17 @@
         return lax.rem(v + 2 * N_CTX, N_CTX)
 
     def inward(i):
-        return side if i % 2 == 0 else -side
+        return side * (1 - 2 * lax.rem(i, 2))
 
     def near(i):
         return ring(t + inward(i) * i)
 
     def head(i):
         return near(i) // 2
+
+    def distance(j):
+        left = lax.rem(2 * j - t + N_CTX, N_CTX)
+        return jnp.where(left < SIDE, left, N_CTX - 1 - left)
 
     def columns(i):
         return pl.ds(pl.multiple_of(head(i) * HD, HD), HD)
@@ -123,10 +136,10 @@
     out_span = jnp.int32(0)
     in_span = jnp.int32(0)
     for i in range(RUNS):
-        mine = offloads_ref[i, 0] == s
-        out_first += jnp.where(mine, offloads_ref[i, 2], 0)
-        out_span += jnp.where(mine, offloads_ref[i, 3] * BLK, 0)
-        in_span += jnp.where(offloads_ref[i, 1] == s, offloads_ref[i, 3] * BLK, 0)
+        mine = offloads_ref[0, i] == s
+        out_first += jnp.where(mine, offloads_ref[2, i], 0)
+        out_span += jnp.where(mine, offloads_ref[3, i] * BLK, 0)
+        in_span += jnp.where(offloads_ref[1, i] == s, offloads_ref[3, i] * BLK, 0)
     count = counts_ref[s]
     length = lengths_ref[s]
     first = jnp.minimum(out_first, 2)
@@ -173,9 +186,9 @@
     def q_arrival(i, o, h):
         return q_partner(h) if i == 0 else q_outward(i - 1, o, h)
 
-    def out_inward(i, h):
+    def out_inward(i, h, o):
         return remote(
-            osend.at[i - 1, h], orecv.at[i - 1, h], o_s.at[i - 1, h], o_r.at[i - 1, h],
+            osend.at[i - 1, h, o], orecv.at[i - 1, h, o], o_s.at[i - 1, h, o], o_r.at[i - 1, h, o],
             (s, ring(t + inward(i))),
         )
 
@@ -191,15 +204,22 @@
         copy.start()
         started.append(copy)
 
-    for h in range(1):
+    def send_kv():
+        for j in KV_TURN:
+            i = distance(j)
+
+            @pl.when(i > REACH)
+            def _():
+                for copy in kv_copies(i):
+                    copy.start()
+
+    def send_queries(h):
         go(q_partner(h))
         go(q_outward(0, 0, h))
-    for i in range(REACH + 1, SIDE):
-        for copy in kv_copies(i):
-            go(copy)
-    for h in range(1, 2):
-        go(q_partner(h))
-        go(q_outward(0, 0, h))
+
+    for h in FIRST_QUERIES:
+        send_queries(h)
+    send_kv()
 
     loads[3].wait()
     loads[4].wait()
@@ -219,12 +239,17 @@
     position = lax.broadcasted_iota(jnp.int32, (2 * N_CTX * 8, 2 * QROWS), 0)
 
     def keep(i, h, state):
-        acc_ref[i, h] = state[0]
-        stat_ref[i, h, 0:1, :] = state[1]
-        stat_ref[i, h, 1:2, :] = state[2]
-
-    def held(i, h):
-        return acc_ref[i, h], stat_ref[i, h, 0:1, :], stat_ref[i, h, 1:2, :]
+        for o in range(2):
+            lo, hi = o * QROWS, (o + 1) * QROWS
+            acc_ref[i, h, o] = state[0][:, lo:hi]
+            stat_ref[i, h, o, 0:1, :] = state[1][:, lo:hi]
+            stat_ref[i, h, o, 1:2, :] = state[2][:, lo:hi]
+
+    def held(i, h, o):
+        return acc_ref[i, h, o], stat_ref[i, h, o, 0:1, :], stat_ref[i, h, o, 1:2, :]
+
+    def held_both(i, h):
+        return tuple(jnp.concatenate(both, axis=1) for both in zip(held(i, h, 0), held(i, h, 1)))
 
     def queries(i, h):
         return jnp.concatenate([qbuf[i, 0, h], qbuf[i, 1, h]], axis=0)
@@ -241,66 +266,75 @@
                 if i < REACH:
                     go(q_outward(i, o, h))
 
-    for step in range(1, REACH + 2):
-        for h in range(2):
-            arrive(step, h)
-            own_block(step - 1, h)
-
-    for i in range(REACH + 1, SIDE):
+    def far_block(i, h):
         slot = i - REACH - 1
-        for copy in kv_copies(i):
-            copy.wait_recv()
+        if h == 0:
+            for copy in kv_copies(i):
+                copy.wait_recv()
+            far_vt[slot] = vbuf[slot].T
         source = ring(t - inward(REACH) * (slot + 1))
-        far_vt = vbuf[slot].T
-        for h in range(2):
-            allowed = position < length - source * 256
-            part = attend(kbuf[slot], far_vt, queries(REACH, h), allowed)
-            keep(REACH, h, merge(held(REACH, h), part))
-
-    for i in range(REACH, 0, -1):
-        for h in range(2):
-            state = held(i, h)
+        allowed = position < length - source * 256
+        part = attend(kbuf[slot], far_vt[slot], queries(REACH, h), allowed)
+        keep(REACH, h, merge(held_both(REACH, h), part))
+
+    def packed(ref, state):
+        ref[:HD, :] = state[0].astype(jnp.bfloat16)
+        ref[HD:PACK, :] = pack_rows(state[1], state[2])
+
+    def out(i, h):
+        for o in (1, 0):
+            state = held(i, h, o)
             if i < REACH:
-                out_inward(i + 1, h).wait_recv()
-                state = merge(state, unpack(orecv[i, h]))
-            osend[i - 1, h, :HD, :] = state[0].astype(jnp.bfloat16)
-            osend[i - 1, h, HD:PACK, :] = pack_rows(state[1], state[2])
-            go(out_inward(i, h))
-    mine = []
-    for h in range(2):
-        out_inward(1, h).wait_recv()
-        acc, top, total = merge(held(0, h), unpack(orecv[0, h]))
-        psend[h, :HD, :] = acc[:, QROWS:].astype(jnp.bfloat16)
-        psend[h, HD:PACK, :] = pack_rows(top[:, QROWS:], total[:, QROWS:])
+                out_inward(i + 1, h, o).wait_recv()
+                state = merge(state, unpack(orecv[i, h, o]))
+            packed(osend.at[i - 1, h, o], state)
+            go(out_inward(i, h, o))
+
+    def pair(h):
+        out_inward(1, h, 1).wait_recv()
+        packed(psend.at[h], merge(held(0, h, 1), unpack(orecv[0, h, 1])))
         go(out_partner(h))
-        keep(0, h, (acc, top, total))
+        out_inward(1, h, 0).wait_recv()
+        own[h] = merge(merge(held(0, h, 0), own[h]), unpack(orecv[0, h, 0]))
 
     def finish(h):
         out_partner(h).wait_recv()
-        acc, top, total = held(0, h)
-        state = merge((acc[:, :QROWS], top[:, :QROWS], total[:, :QROWS]), own[h])
-        acc, top, total = merge(state, unpack(precv[h]))
+        acc, top, total = merge(own[h], unpack(precv[h]))
         rows = (acc / total).T
         for n in range(4):
             for part in range(2):
                 lo = n * HALF + part * BLK
                 fin_f[2 * h + part, :, n * HD : (n + 1) * HD] = rows[lo : lo + BLK]
 
+    actions = {
+        "queries": send_queries, "arrive": arrive, "own": own_block, "far": far_block, "out": out, "pair": pair,
+    }
+    for name, *which in SCHEDULE:
+        actions[name](*which)
     finish(0)
     shifted = out_first > first
     run[:BLK, :] = jnp.where(shifted, fin_f[1], fin_f[0]).astype(jnp.bfloat16)
     run[BLK:, :] = fin_f[1].astype(jnp.bfloat16)
 
+    def chip_at(k, sign):
+        dx, dy = OFFSETS[k]
+        return lax.rem(chip // 4 + 4 + sign * dx, 4) * 4 + lax.rem(lax.rem(chip, 4) + 4 + sign * dy, 4)
+
+    def piece(ref, i):
+        rows = pl.ds(pl.multiple_of((i // 4) * 16, 16), 16)
+        return ref.at[rows, pl.ds(pl.multiple_of(lax.rem(i, 4) * HD, HD), HD)]
+
     def p1_copy(k):
-        there = lax.rem(chip + k, CHIPS)
-        piece = run.at[
-            pl.ds(pl.multiple_of((there // 4) * 16, 16), 16), pl.ds(pl.multiple_of(lax.rem(there, 4) * HD, HD), HD)
-        ]
-        return remote(piece, p1.at[core * CHIPS + chip], p1_s.at[k], p1_r.at[k], (2 * there + core, t))
+        there = chip_at(k, 1)
+        return remote(
+            piece(run, there), p1.at[core * CHIPS + chip], p1_s.at[k], p1_r.at[k], (2 * there + core, t)
+        )
 
     def p1_arrival(k):
-        here = lax.rem(chip + CHIPS - k, CHIPS)
-        return remote(p1.at[core * CHIPS + here], p1.at[core * CHIPS + here], p1_s.at[k], p1_r.at[k], (2 * here + core, t))
+        here = chip_at(k, -1)
+        return remote(
+            p1.at[core * CHIPS + here], p1.at[core * CHIPS + here], p1_s.at[k], p1_r.at[k], (2 * here + core, t)
+        )
 
     my_rows = pl.ds(pl.multiple_of((chip // 4) * 16, 16), 16)
     my_cols = pl.ds(pl.multiple_of(lax.rem(chip, 4) * HD, HD), HD)
@@ -308,17 +342,13 @@
         go(p1_copy(k))
     p1[core * CHIPS + chip] = run[my_rows, my_cols]
 
-    finish(1)
-    row32 = lax.broadcasted_iota(jnp.int32, (BLK, 4 * HD), 0)
-    for b in range(4):
-        place = jnp.where(
-            first == b, 0, jnp.where(first + 1 == b, 1, jnp.where(rest_a == b, 2, 3))
-        )
-        rows = fin_f[place]
-        row = row32 + b * BLK
-        retained = (row < count) & ((row < out_start) | (row >= out_start + out_span))
-        mixed_ref[b * BLK : (b + 1) * BLK, :] = jnp.where(retained, rows, 0.0).astype(jnp.bfloat16)
-
+    for name, *which in LATE:
+        actions[name](*which)
+    slots = [lax.rem(offloads_ref[0, i], 2) * CHIPS + lax.div(offloads_ref[0, i], 2) for i in range(RUNS)]
+    wanted = []
+    for k in range(CHIPS):
+        target = 2 * chip_at(k, 1) + core
+        wanted.append(sum(jnp.where(offloads_ref[1, i] == target, slots[i], 0) for i in range(RUNS)))
     for k in range(1, CHIPS):
         p1_arrival(k).wait_recv()
     mine16 = p1.at[pl.ds(core * CHIPS, CHIPS)]
@@ -328,34 +358,40 @@
     other.wait_recv()
 
     def p3_copy(k):
-        there = lax.rem(chip + k, CHIPS)
-        return remote(p3.at[k], host.at[my_rows, my_cols], p3_s.at[k], p3_r.at[k], (2 * there + core, t))
+        there = chip_at(k, 1)
+        return remote(p3.at[k], piece(host, chip), p3_s.at[k], p3_r.at[k], (2 * there + core, t))
 
     def p3_arrival(k):
-        here = lax.rem(chip + CHIPS - k, CHIPS)
-        place = host.at[
-            pl.ds(pl.multiple_of((here // 4) * 16, 16), 16), pl.ds(pl.multiple_of(lax.rem(here, 4) * HD, HD), HD)
-        ]
-        return remote(place, place, p3_s.at[k], p3_r.at[k], (2 * here + core, t))
-
-    slots = [lax.rem(offloads_ref[i, 0], 2) * CHIPS + lax.div(offloads_ref[i, 0], 2) for i in range(RUNS)]
-    for k in range(CHIPS):
-        target = 2 * lax.rem(chip + k, CHIPS) + core
-        source = jnp.int32(0)
-        for i in range(RUNS):
-            source += jnp.where(offloads_ref[i, 1] == target, slots[i], 0)
-        piece = p1[source]
-        if k == 0:
-            host[my_rows, my_cols] = piece
-        else:
-            p3[k] = piece
-            go(p3_copy(k))
+        here = chip_at(k, -1)
+        return remote(piece(host, here), piece(host, here), p3_s.at[k], p3_r.at[k], (2 * here + core, t))
+
+    for k in range(1, CHIPS):
+        p3[k] = p1[wanted[k]]
+        go(p3_copy(k))
+    host[my_rows, my_cols] = p1[wanted[0]]
+    finish(1)
+    row32 = lax.broadcasted_iota(jnp.int32, (BLK, 4 * HD), 0)
+    for b in range(4):
+        place = jnp.where(
+            first == b, 0, jnp.where(first + 1 == b, 1, jnp.where(rest_a == b, 2, 3))
+        )
+        rows = fin_f[place]
+        row = row32 + b * BLK
+        retained = (row < count) & ((row < out_start) | (row >= out_start + out_span))
+        mixed_ref[b * BLK : (b + 1) * BLK, :] = jnp.where(retained, rows, 0.0).astype(jnp.bfloat16)
+
+    passed = started[-(CHIPS - 1) :]
+    for copy in started[: -(CHIPS - 1)]:
+        copy.wait_send()
+    for i in range(REACH + 1, SIDE):
+        for copy in kv_copies(i):
+            copy.wait_send()
     for k in range(1, CHIPS):
         p3_arrival(k).wait_recv()
     row64 = lax.broadcasted_iota(jnp.int32, (CAP, 4 * HD), 0)
     hosted_ref[...] = jnp.where(row64 < in_span, host[...].astype(jnp.float32), 0.0).astype(jnp.bfloat16)
 
-    for copy in started:
+    for copy in passed:
         copy.wait_send()
 
 
@@ -387,10 +423,11 @@
             pltpu.VMEM((REACH + 1, 2, 2, QROWS, HD), bf16),
             pltpu.VMEM((far, 256, HD), bf16),
             pltpu.VMEM((far, 256, HD), bf16),
-            pltpu.VMEM((REACH + 1, 2, HD, 2 * QROWS), f32),
-            pltpu.VMEM((REACH + 1, 2, 8, 2 * QROWS), f32),
-            pltpu.VMEM((REACH, 2, PACK, 2 * QROWS), bf16),
-            pltpu.VMEM((REACH, 2, PACK, 2 * QROWS), bf16),
+            pltpu.VMEM((far, HD, 256), bf16),
+            pltpu.VMEM((REACH + 1, 2, 2, HD, QROWS), f32),
+            pltpu.VMEM((REACH + 1, 2, 2, 8, QROWS), f32),
+            pltpu.VMEM((REACH, 2, 2, PACK, QROWS), bf16),
+            pltpu.VMEM((REACH, 2, 2, PACK, QROWS), bf16),
             pltpu.VMEM((2, PACK, QROWS), bf16),
             pltpu.VMEM((2, PACK, QROWS), bf16),
             pltpu.VMEM((4, BLK, 4 * HD), f32),
@@ -403,8 +440,8 @@
             dma((2, far)),
             dma((REACH + 1, 3, 2)),
             dma((REACH + 1, 2, 2)),
-            dma((REACH, 2)),
-            dma((REACH, 2)),
+            dma((REACH, 2, 2)),
+            dma((REACH, 2, 2)),
             dma((2,)),
             dma((2,)),
             dma((CHIPS,)),
@@ -415,9 +452,9 @@
             dma((CHIPS,)),
         ],
         compiler_params=pltpu.CompilerParams(
-            collective_id=0, has_side_effects=True, vmem_limit_bytes=48 * 1024 * 1024
+            collective_id=0, has_side_effects=True, vmem_limit_bytes=60 * 1024 * 1024
         ),
-    )(new_counts, ctx_lengths, offloads, new_queries.reshape(4, BLK, 4 * HD), new_keys, new_values, cache_keys, cache_values)
+    )(new_counts, ctx_lengths, offloads.T, new_queries.reshape(4, BLK, 4 * HD), new_keys, new_values, cache_keys, cache_values)
 
 
 def solution(mesh):

time: 87.9 us -> 77.9 us (0.89)
  the two profiles are of different devices: /device:TPU:1 before, /device:TPU:33 now
where the time goes in v2:
time: 77.9 us; the launch traced here: 77.7 us
  Pallas kernels  74.8 us (96%)
  local copies, waits for them, and re-layouts  2.23 us (3%)
    pallas_call x1, Pallas kernels, local(): pl.pallas_call(kernel, name='attend_and_relocate', out_shape=(jax.ShapeDt...  74.8 us
    unnamed x4, local copies, waits for them, and re-layouts  2.23 us

profile of v2, /device:TPU:33, one launch (start us, length us, event | category | flops | bytes accessed | tf_op | source)
XLA Modules:
  0.0 77.7 jit_solution(17673985092869326648)
XLA Ops:
  0.6 74.8 %attend_and_relocate.1 = (bf16[128,512]{1,0:T(8,128)(2,1)}, bf16[64,512]{1,0:T(8,128)(2,1)}) custom-call(s32[32]{0:T(128)} %counts_ref.1, s32[32]{0:T(128)} %lengths_ref.1, s32[4,8]{1,0:T(4,128)} %bitcast.3, bf16[4,32,512]{2,1,0:T(8,128)(2,1)} %bitcast.2, bf16[128,1024]{1,0:T(8,128)(2,1)} %nk_hbm.1, bf16[128,1024]{1,0:T(8,128)(2,1)} %nv_hbm.1, ...), custom_call_target="tpu_custom_call" | custom-call | tf_op jit(solution)/shard_map/attend_and_relocate/pallas_call | solution.py:407
  75.5 0.0 copy-start
  75.5 1.6 %copy.12 = bf16[128,512]{1,0:T(8,128)(2,1)} copy(bf16[128,512]{1,0:T(8,128)(2,1)} %get-tuple-element.4) | data formatting | bytes 262144
  77.1 0.0 copy-done
  77.1 0.6 copy.13
Async XLA Ops:
  75.5 1.6 %copy-start = (bf16[64,512]{1,0:T(8,128)(2,1)S(1)}, bf16[64,512]{1,0:T(8,128)(2,1)}, u32[]{:S(2)}) copy-start(bf16[64,512]{1,0:T(8,128)(2,1)} %get-tuple-element.5) | copy-start | bytes 196612

commit v3 on v2

--- a/solution.py
+++ b/solution.py
@@ -21,7 +21,7 @@
 SIDE = N_CTX // 2
 REACH = 1
 FAR = SIDE - 1 - REACH
-KV_TURN = (0, 1, 2, 3, 4, 5, 6, 7)
+KV_TURN = ((0, 1, 7, 2, 3, 4, 5, 6),)
 OFFSETS = sorted(
     ((dx, dy) for dx in range(4) for dy in range(4)),
     key=lambda d: -(min(d[0], 4 - d[0]) + min(d[1], 4 - d[1])),
@@ -35,7 +35,7 @@
 LOG2_SCALE = math.log2(math.e) / math.sqrt(HD)
 MESH = pl.DeviceIdType.MESH
 FIRST_QUERIES = (0, 1)
-SCHEDULE = (('arrive', 1, 0), ('arrive', 1, 1), ('own', 0, 0), ('own', 0, 1), ('arrive', 2, 0), ('arrive', 2, 1), ('own', 1, 0), ('own', 1, 1), ('far', 2, 0), ('far', 2, 1), ('far', 3, 0), ('far', 3, 1), ('far', 4, 0), ('far', 4, 1), ('far', 5, 0), ('far', 5, 1), ('far', 6, 0), ('far', 6, 1), ('far', 7, 0), ('out', 1, 0), ('far', 7, 1), ('out', 1, 1), ('pair', 0))
+SCHEDULE = (('arrive', 1, 0), ('arrive', 1, 1), ('own', 0, 0), ('own', 0, 1), ('arrive', 2, 0), ('arrive', 2, 1), ('own', 1, 0), ('own', 1, 1), ('far', 2, 0), ('far', 3, 0), ('far', 4, 0), ('far', 5, 0), ('far', 6, 0), ('far', 7, 0), ('out', 1, 0), ('far', 2, 1), ('far', 3, 1), ('far', 4, 1), ('far', 5, 1), ('far', 6, 1), ('far', 7, 1), ('out', 1, 1), ('pair', 0))
 LATE = (('pair', 1),)
 
 
@@ -204,8 +204,8 @@
         copy.start()
         started.append(copy)
 
-    def send_kv():
-        for j in KV_TURN:
+    def send_kv(turn):
+        for j in KV_TURN[turn]:
             i = distance(j)
 
             @pl.when(i > REACH)
@@ -219,7 +219,7 @@
 
     for h in FIRST_QUERIES:
         send_queries(h)
-    send_kv()
+    send_kv(0)
 
     loads[3].wait()
     loads[4].wait()
@@ -307,7 +307,7 @@
                 fin_f[2 * h + part, :, n * HD : (n + 1) * HD] = rows[lo : lo + BLK]
 
     actions = {
-        "queries": send_queries, "arrive": arrive, "own": own_block, "far": far_block, "out": out, "pair": pair,
+        "queries": send_queries, "kv": send_kv, "arrive": arrive, "own": own_block, "far": far_block, "out": out, "pair": pair,
     }
     for name, *which in SCHEDULE:
         actions[name](*which)

time: 77.9 us -> 76.6 us (0.983)
  the two profiles are of different devices: /device:TPU:33 before, /device:TPU:1 now
where the time goes in v3:
time: 76.6 us; the launch traced here: 76.4 us
  Pallas kernels  73.5 us (96%)
  local copies, waits for them, and re-layouts  2.23 us (3%)
    pallas_call x1, Pallas kernels, local(): pl.pallas_call(kernel, name='attend_and_relocate', out_shape=(jax.ShapeDt...  73.5 us
    unnamed x4, local copies, waits for them, and re-layouts  2.23 us

profile of v3, /device:TPU:1, one launch (start us, length us, event | category | flops | bytes accessed | tf_op | source)
XLA Modules:
  0.0 76.4 jit_solution(2739914116049579328)
XLA Ops:
  0.6 73.5 %attend_and_relocate.1 = (bf16[128,512]{1,0:T(8,128)(2,1)}, bf16[64,512]{1,0:T(8,128)(2,1)}) custom-call(s32[32]{0:T(128)} %counts_ref.1, s32[32]{0:T(128)} %lengths_ref.1, s32[4,8]{1,0:T(4,128)} %bitcast.3, bf16[4,32,512]{2,1,0:T(8,128)(2,1)} %bitcast.2, bf16[128,1024]{1,0:T(8,128)(2,1)} %nk_hbm.1, bf16[128,1024]{1,0:T(8,128)(2,1)} %nv_hbm.1, ...), custom_call_target="tpu_custom_call" | custom-call | tf_op jit(solution)/shard_map/attend_and_relocate/pallas_call | solution.py:407
  74.2 0.0 copy-start
  74.2 1.6 %copy.12 = bf16[128,512]{1,0:T(8,128)(2,1)} copy(bf16[128,512]{1,0:T(8,128)(2,1)} %get-tuple-element.4) | data formatting | bytes 262144
  75.8 0.0 copy-done
  75.8 0.6 copy.13
Async XLA Ops:
  74.2 1.6 %copy-start = (bf16[64,512]{1,0:T(8,128)(2,1)S(1)}, bf16[64,512]{1,0:T(8,128)(2,1)}, u32[]{:S(2)}) copy-start(bf16[64,512]{1,0:T(8,128)(2,1)} %get-tuple-element.5) | copy-start | bytes 196612
